TPU v7x, 256 devices: a whole 4x4x8 slice. The times are simulated.
256 devices in a mesh: tensor: 4 (over x), expert: 32 (over y, z), dp: 2 (over core).
Axes of the slice: x: 4, y: 4, z: 8, core: 2. Of those that a mesh axis runs over, the one named last changes fastest.
Arguments:
- tokens: bfloat16 [16384, 2048], P(('expert', 'dp')), may hold values from -6 to 6
- grad_output: bfloat16 [16384, 2048], P(('expert', 'dp')), may hold values from -4 to 4
- gate_prob: float32 [16384], P(('expert', 'dp')), may hold values from 0.3 to 1
- expert_index: int32 [16384, 1], P(('expert', 'dp')), may hold values from 0 to 31, as said below
- slot_index: int32 [16384, 1], P(('expert', 'dp')), may hold values from 0 to 15, as said below
- up_weight: bfloat16 [32, 2048, 4096], P('expert', 'dp', 'tensor'), may hold values from -0.125 to 0.125
- down_weight: bfloat16 [32, 2048, 4096], P('expert', 'dp', 'tensor'), may hold values from -0.09375 to 0.09375
Outputs:
- grad_tokens: bfloat16 [16384, 2048], P(('expert', 'dp'), 'tensor')
- grad_up: bfloat16 [32, 2048, 4096], P('expert', 'dp', 'tensor')
- grad_down: bfloat16 [32, 2048, 4096], P('expert', 'dp', 'tensor')
Inputs may be any that keep to these rules, and one draw needn't show every extreme that they name: `expert_index`: within each aligned block of 256 rows, at most 16 rows choose one expert; in every block one expert is chosen by exactly 16 rows, and other experts by varying numbers. `slot_index`: slots of rows that choose the same expert within an aligned block of 256 rows are distinct.
All inputs are finite; a program needn't handle non-finite values.
Results may differ from a plain program's by a relative error of at most 0.015.
Values may be sent and summed in bfloat16 or wider, within the bound.
A program may use at most 128 MiB of HBM per device.

v0:
```python
import jax
import jax.numpy as jnp
from jax import lax
from jax.sharding import PartitionSpec as P


def expert_grads(token_rows, grad_rows, up_matrix, down_matrix):
    pre_act = jnp.dot(token_rows, up_matrix, preferred_element_type=jnp.float32)
    hidden = jax.nn.gelu(pre_act).astype(jnp.bfloat16)
    hidden_grad = jnp.dot(grad_rows, down_matrix, preferred_element_type=jnp.float32)
    slope_grad = jax.vjp(jax.nn.gelu, pre_act)[1](hidden_grad)[0].astype(jnp.bfloat16)
    input_part = lax.dot_general(
        slope_grad, up_matrix, (((1,), (1,)), ((), ())), preferred_element_type=jnp.float32
    )
    return (hidden, slope_grad, input_part)


def local(tokens, grad_output, gate_prob, expert_index, slot_index, up_weight, down_weight):
    experts = lax.axis_size("expert")
    tensor_size = lax.axis_size("tensor")
    tok_count = tokens.shape[0]
    model_width = tokens.shape[1]
    capacity = 2 * tok_count // experts
    feature_share = model_width // tensor_size
    position = expert_index[:, 0] * capacity + slot_index[:, 0]
    onehot = (
        lax.broadcasted_iota(jnp.int32, (experts * capacity, tok_count), 0) == position[None, :]
    ).astype(jnp.bfloat16)
    scaled = (grad_output.astype(jnp.float32) * gate_prob[:, None]).astype(jnp.bfloat16)
    up_full, down_full = (
        lax.all_gather(up_weight, "dp", axis=1, tiled=True),
        lax.all_gather(down_weight, "dp", axis=1, tiled=True),
    )
    up_full = up_full[0]
    down_full = down_full[0]

    def dispatch(columns):
        placed = jnp.dot(onehot, columns, preferred_element_type=jnp.float32).astype(jnp.bfloat16)
        return placed.reshape(experts, capacity, columns.shape[1])

    token_buf, grad_buf = (
        lax.all_to_all(dispatch(tokens), "expert", split_axis=0, concat_axis=0, tiled=True),
        lax.all_to_all(dispatch(scaled), "expert", split_axis=0, concat_axis=0, tiled=True),
    )
    rows_total = token_buf.shape[0] * capacity
    token_rows = token_buf.reshape(rows_total, model_width)
    grad_rows = grad_buf.reshape(rows_total, model_width)
    hidden, slope_grad, input_part = expert_grads(token_rows, grad_rows, up_full, down_full)
    columns = grad_rows
    grad_down = lax.psum_scatter(
        lax.dot_general(
            columns, hidden, (((0,), (0,)), ((), ())), preferred_element_type=jnp.float32
        ).astype(jnp.bfloat16),
        "dp",
        scatter_dimension=0,
        tiled=True,
    ).astype(jnp.float32)
    columns = token_rows
    grad_up = lax.psum_scatter(
        lax.dot_general(
            columns, slope_grad, (((0,), (0,)), ((), ())), preferred_element_type=jnp.float32
        ).astype(jnp.bfloat16),
        "dp",
        scatter_dimension=0,
        tiled=True,
    ).astype(jnp.float32)
    share_sums = lax.psum_scatter(
        input_part.reshape(experts, capacity, model_width).astype(jnp.bfloat16),
        "tensor",
        scatter_dimension=2,
        tiled=True,
    )
    returned = lax.all_to_all(share_sums, "expert", split_axis=0, concat_axis=0, tiled=True)
    grad_tokens = lax.dot_general(
        onehot,
        returned.reshape(experts * capacity, feature_share),
        (((0,), (0,)), ((), ())),
        preferred_element_type=jnp.float32,
    )
    return (
        grad_tokens.astype(jnp.bfloat16),
        grad_up[None].astype(jnp.bfloat16),
        grad_down[None].astype(jnp.bfloat16),
    )


def solution(mesh):
    placed = (
        P(("expert", "dp"), None),
        P(("expert", "dp"), None),
        P(("expert", "dp")),
        P(("expert", "dp"), None),
        P(("expert", "dp"), None),
        P("expert", "dp", "tensor"),
        P("expert", "dp", "tensor"),
    )
    return jax.shard_map(
        local,
        mesh=mesh,
        in_specs=placed,
        out_specs=(
            P(("expert", "dp"), "tensor"),
            P("expert", "dp", "tensor"),
            P("expert", "dp", "tensor"),
        ),
        check_vma=False,
    )
```

profile of v0, /device:TPU:4, one launch (start us, length us, event | category | flops | bytes accessed | tf_op | source)
XLA Modules:
  0.0 218.6 jit_solution(3057496867985842111)
XLA Ops:
  7.2 0.0 copy-start
  7.2 0.0 all-gather.5.cloned.1.call-start
  7.2 0.7 all-gather.5.cloned.1.call-update
  7.9 0.0 copy-done.2
  7.9 0.0 copy-done.3
  8.0 0.5 copy-done
  8.4 2.0 convolution_convert_fusion.2
  10.5 11.6 %all-to-all-start.1 = ((bf16[32,16,2048]{2,1,0:T(8,128)(2,1)}), bf16[32,16,2048]{2,1,0:T(8,128)(2,1)S(1)}, u32[]{:S(2)}, u32[]{:S(2)}) async-start(bf16[32,16,2048]{2,1,0:T(8,128)(2,1)} %bitcast.4), calls=%async_computation.1 | async-start | bytes 4194304 | tf_op jit(solution)/shard_map/all_to_all | solution.py:42
  22.1 0.0 all-gather.3.cloned.1.call-start
  22.1 0.7 all-gather.3.cloned.1.call-update
  22.9 3.4 %convolution_convert_fusion.3 = bf16[512,2048]{1,0:T(8,128)(2,1)} fusion(bf16[256,2048]{1,0:T(8,128)(2,1)} %param.8, f32[256]{0:T(256)S(1)} %copy-done.1, s32[256]{0:T(256)S(1)} %bitcast.34), kind=kOutput, calls=%fused_computation.12 | convolution fusion | flops 539623424 | bytes 3147776 | tf_op jit(solution)/shard_map/dot_general | solution.py:38
  26.3 45.8 %all-to-all-done.1 = bf16[32,16,2048]{2,1,0:T(8,128)(2,1)S(1)} async-done(((bf16[32,16,2048]{2,1,0:T(8,128)(2,1)}), bf16[32,16,2048]{2,1,0:T(8,128)(2,1)S(1)}, u32[]{:S(2)}, u32[]{:S(2)}) %all-to-all-start.1) | async-done | bytes 2097184 | tf_op jit(solution)/shard_map/all_to_all | solution.py:42
  72.1 6.3 %all-to-all-start = ((bf16[32,16,2048]{2,1,0:T(8,128)(2,1)}), bf16[32,16,2048]{2,1,0:T(8,128)(2,1)}, u32[]{:S(2)}, u32[]{:S(2)}) async-start(bf16[32,16,2048]{2,1,0:T(8,128)(2,1)} %bitcast.1), calls=%async_computation | async-start | bytes 4194304 | tf_op jit(solution)/shard_map/all_to_all | solution.py:43
  78.4 0.0 reduce-scatter.4.cloned.1.call-start
  78.5 0.0 all-gather.5.cloned.1.call-done
  78.5 5.9 %fusion.2 = f32[512,1024]{1,0:T(8,128)} fusion(bf16[512,2048]{1,0:T(8,128)(2,1)S(1)} %bitcast.30, bf16[1,2048,1024]{2,1,0:T(8,128)(2,1)} %all-gather.5.cloned.1.call-done), kind=kOutput, calls=%fused_computation.2 | convolution fusion | flops 2147483648 | bytes 8388608 | tf_op jit(solution)/shard_map/dot_general | solution.py:8
  84.4 43.8 %all-to-all-done = bf16[32,16,2048]{2,1,0:T(8,128)(2,1)} async-done(((bf16[32,16,2048]{2,1,0:T(8,128)(2,1)}), bf16[32,16,2048]{2,1,0:T(8,128)(2,1)}, u32[]{:S(2)}, u32[]{:S(2)}) %all-to-all-start) | async-done | bytes 2097184 | tf_op jit(solution)/shard_map/all_to_all | solution.py:43
  128.2 7.0 %fusion.15 = bf16[512,1024]{1,0:T(8,128)(2,1)S(1)} fusion(f32[512,1024]{1,0:T(8,128)} %fusion.2, bf16[512,2048]{1,0:T(8,128)(2,1)} %bitcast.2, bf16[1,2048,1024]{2,1,0:T(8,128)(2,1)} %all-gather.3.cloned.1.call-done), kind=kOutput, calls=%fused_computation.19 | convolution fusion | flops 2157969408 | bytes 9437184 | tf_op jit(solution)/shard_map/dot_general | solution.py:10
  135.2 1.0 copy-done.5
  136.1 3.7 %fusion.6 = bf16[32,16,2048]{2,1,0:T(8,128)(2,1)} fusion(bf16[32,16,1024]{2,1,0:T(8,128)(2,1)S(1)} %bitcast.38, bf16[1,2048,1024]{2,1,0:T(8,128)(2,1)S(1)} %copy-done.4), kind=kOutput, calls=%fused_computation.10 | convolution fusion | flops 2148532224 | bytes 7340032 | tf_op jit(solution)/shard_map/dot_general | solution.py:12
  139.8 0.0 reduce-scatter.4.cloned.1.call-update
  139.8 0.0 reduce-scatter.6.cloned.1.call-start
  139.9 5.6 %convolution_convert_fusion.1 = bf16[2048,1024]{1,0:T(8,128)(2,1)} fusion(bf16[512,2048]{1,0:T(8,128)(2,1)S(1)} %bitcast.31, bf16[512,1024]{1,0:T(8,128)(2,1)} %copy-done.5), kind=kOutput, calls=%fused_computation.7 | convolution fusion | flops 2149580800 | bytes 7340032 | tf_op jit(solution)/shard_map/dot_general | solution.py:60
  145.5 0.0 reduce-scatter.6.cloned.1.call-update
  145.5 0.2 reduce-scatter.8.cloned.1.call-start
  145.7 1.3 copy-done.6
  147.1 6.1 %convolution_convert_fusion = bf16[2048,1024]{1,0:T(8,128)(2,1)} fusion(bf16[512,2048]{1,0:T(8,128)(2,1)} %bitcast.2, f32[512,1024]{1,0:T(8,128)S(1)} %copy-done.6), kind=kOutput, calls=%fused_computation.6 | convolution fusion | flops 2154299392 | bytes 8388608 | tf_op jit(solution)/shard_map/dot_general | solution.py:51
  153.2 0.0 reduce-scatter.8.cloned.1.call-update
  153.2 15.0 %reduce-scatter.4.cloned.1.call-done = bf16[32,16,512]{2,1,0:T(8,128)(2,1)} async-done(((bf16[32,16,2048]{2,1,0:T(8,128)(2,1)}), bf16[32,16,512]{2,1,0:T(8,128)(2,1)}) %reduce-scatter.4.cloned.1.call-update) | async-done | bytes 524304 | tf_op jit(solution)/shard_map/reduce_scatter | solution.py:67
  168.3 26.6 %all_to_all.15 = bf16[32,16,512]{2,1,0:T(8,128)(2,1)S(1)} all-to-all(bf16[32,16,512]{2,1,0:T(8,128)(2,1)} %reduce-scatter.4.cloned.1.call-done), channel_id=1, replica_groups=mesh['tensor'=4,'expert'=32,'dp'=2] {'expert'}, dimensions={0} | all-to-all | bytes 1048576 | tf_op jit(solution)/shard_map/all_to_all | solution.py:73
  194.9 1.1 convolution_convert_fusion.4
  195.9 16.1 %reduce-scatter.8.cloned.1.call-done = bf16[1024,1024]{1,0:T(8,128)(2,1)} async-done(((bf16[2048,1024]{1,0:T(8,128)(2,1)}), bf16[1024,1024]{1,0:T(8,128)(2,1)}) %reduce-scatter.8.cloned.1.call-update) | async-done | bytes 2097168 | tf_op jit(solution)/shard_map/reduce_scatter | solution.py:50
  (11 shorter events, 0.0 us)
Async XLA Ops:
  7.2 1.3 copy-start
  7.2 0.8 copy-start.2
  7.2 0.8 copy-start.3
  7.2 71.3 %all-gather.5.cloned.1.call-start = ((), (), s32[]{:S(2)}) async-start(), calls=%async_computation.7 | async-start | bytes 6291456 | tf_op jit(solution)/shard_map/all_gather | solution.py:31
  10.5 12.4 %copy-start.1 = (f32[256]{0:T(256)S(1)}, f32[256]{0:T(256)}, u32[]{:S(2)}) copy-start(f32[256]{0:T(256)} %param.9) | copy-start | bytes 3076
  10.5 61.7 %all-to-all-start.1 = ((bf16[32,16,2048]{2,1,0:T(8,128)(2,1)}), bf16[32,16,2048]{2,1,0:T(8,128)(2,1)S(1)}, u32[]{:S(2)}, u32[]{:S(2)}) async-start(bf16[32,16,2048]{2,1,0:T(8,128)(2,1)} %bitcast.4), calls=%async_computation.1 | async-start | bytes 4194304 | tf_op jit(solution)/shard_map/all_to_all | solution.py:42
  22.1 106.1 %all-gather.3.cloned.1.call-start = ((), (), s32[]{:S(2)}) async-start(), calls=%async_computation.6 | async-start | bytes 6291456 | tf_op jit(solution)/shard_map/all_gather | solution.py:32
  72.1 56.0 %all-to-all-start = ((bf16[32,16,2048]{2,1,0:T(8,128)(2,1)}), bf16[32,16,2048]{2,1,0:T(8,128)(2,1)}, u32[]{:S(2)}, u32[]{:S(2)}) async-start(bf16[32,16,2048]{2,1,0:T(8,128)(2,1)} %bitcast.1), calls=%async_computation | async-start | bytes 4194304 | tf_op jit(solution)/shard_map/all_to_all | solution.py:43
  78.4 89.8 %reduce-scatter.4.cloned.1.call-start = ((), (), s32[]{:S(2)}) async-start(), calls=%async_computation.8 | async-start | bytes 2621440 | tf_op jit(solution)/shard_map/reduce_scatter | solution.py:67
  128.2 8.0 %copy-start.4 = (bf16[1,2048,1024]{2,1,0:T(8,128)(2,1)S(1)}, bf16[1,2048,1024]{2,1,0:T(8,128)(2,1)}, u32[]{:S(2)}) copy-start(bf16[1,2048,1024]{2,1,0:T(8,128)(2,1)} %all-gather.5.cloned.1.call-done) | copy-start | bytes 12582916
  135.1 1.0 copy-start.5
  139.8 56.1 %reduce-scatter.6.cloned.1.call-start = ((), (), s32[]{:S(2)}) async-start(), calls=%async_computation.9 | async-start | bytes 6291456 | tf_op jit(solution)/shard_map/reduce_scatter | solution.py:59
  145.5 1.6 copy-start.6
  145.5 66.5 %reduce-scatter.8.cloned.1.call-start = ((), (), s32[]{:S(2)}) async-start(), calls=%async_computation.10 | async-start | bytes 6291456 | tf_op jit(solution)/shard_map/reduce_scatter | solution.py:50
Sparse Core Ops, SparseCore 0:
  9.8 21.9 all-gather.4
  33.6 20.2 all-gather.2
  140.0 28.2 reduce-scatter.3
  171.4 18.7 reduce-scatter.5
  193.2 18.8 reduce-scatter.7
where the time goes:
time: 220 us; the launch traced here: 219 us
  waiting for transfers between devices  122 us (55%)
  matrix products  34.8 us (16%)
  blocking collectives  26.6 us (12%)
  starting transfers between devices  18.3 us (8%)
  between operations  13.9 us (6%)
  local copies, waits for them, and re-layouts  2.81 us (1%)
    all_to_all x1, waiting for transfers between devices, local(): lax.all_to_all(dispatch(tokens), 'expert', split_axis=0, concat_axis=0, t...  45.8 us
    all_to_all x1, waiting for transfers between devices, local(): lax.all_to_all(dispatch(scaled), 'expert', split_axis=0, concat_axis=0, t...  43.8 us
    all_to_all x1, blocking collectives, local(): lax.all_to_all(share_sums, 'expert', split_axis=0, concat_axis=0, tiled=T...  26.6 us
    reduce_scatter x1, waiting for transfers between devices, local(): lax.psum_scatter(lax.dot_general(columns, hidden, (((0,), (0,)), ((), ())...  16.1 us
    reduce_scatter x1, waiting for transfers between devices, local(): lax.psum_scatter(input_part.reshape(experts, capacity, model_width).astyp...  15 us
    all_to_all x1, starting transfers between devices, local(): lax.all_to_all(dispatch(tokens), 'expert', split_axis=0, concat_axis=0, t...  11.6 us
    dot_general x1, matrix products, expert_grads(): jnp.dot(grad_rows, down_matrix, preferred_element_type=jnp.float32)  6.98 us
    all_to_all x1, starting transfers between devices, local(): lax.all_to_all(dispatch(scaled), 'expert', split_axis=0, concat_axis=0, t...  6.26 us
  transfers between devices with their start and end apart: 7, of which 4 were waited for; matrix products, arithmetic and copies ran while one was open for 11% of the time, Pallas kernels for 0%

commit v1 on v0

v1 whole, which is shorter than its diff:
```python
import jax
import jax.numpy as jnp
from jax import lax
from jax.experimental import pallas as pl
from jax.experimental.pallas import tpu as pltpu
from jax.sharding import PartitionSpec as P

MESH = pl.DeviceIdType.MESH
F32 = jnp.float32
BF16 = jnp.bfloat16
ROOT = 0.7978845608028654
CUBE = 0.044715

NY, NZ, NX = 4, 8, 4
CAP = 16
NS = NY * NZ
QUARTER = 512
PAIRS = 4


def dot(a, b, dims):
    return lax.dot_general(a, b, (dims, ((), ())), preferred_element_type=F32)


def activation(pre, back):
    square = pre * pre
    bent = jnp.tanh(ROOT * (pre + CUBE * (pre * square)))
    share = 0.5 * (1.0 + bent)
    slope = share + pre * (0.5 * (1.0 - bent * bent)) * (ROOT * (1.0 + 3.0 * CUBE * square))
    return (pre * share).astype(BF16), (back * slope).astype(BF16)


def kernel(
    pos_ref, gate_ref, tok_hbm, gout_hbm, up_hbm, down_hbm,
    ret, gu_out, gd_out,
    tokv, goutv, near, far, rows, prows, up, down, hs, phs, inp, ra, rb, rp, rm, res, gu, gd,
    load_sem, near_send, far_send, yz_recv, own_send, plus_recv, minus_recv, fwd_send, fplus_recv, fminus_recv,
    w_send, w_recv, dp_send, prow_recv, phs_recv,
    first_send, ra_recv, rb_recv, second_send, rp_recv, rm_recv, ret_send, ret_recv, out_sem,
):
    t = lax.axis_index("tensor")
    e = lax.axis_index("expert")
    d = lax.axis_index("dp")
    y, z = e // NZ, e % NZ
    left, right, across = (t + 3) % NX, (t + 1) % NX, (t + 2) % NX
    other = 1 - d

    def at_offset(s, sign):
        k, dy = s // NY, s % NY
        dz = ((k + 1) // 2) * (2 * (k % 2) - 1)
        return (t, ((y + sign * dy + NY) % NY) * NZ + (z + sign * dz + NZ) % NZ, d)

    right_dev, left_dev, other_dev = (right, e, d), (left, e, d), (t, e, other)

    def remote(src, dst, send, recv, dev):
        return pltpu.make_async_remote_copy(
            src_ref=src, dst_ref=dst, send_sem=send, recv_sem=recv, device_id=dev, device_id_type=MESH
        )

    loads = [
        pltpu.make_async_copy(tok_hbm, tokv, load_sem.at[0]),
        pltpu.make_async_copy(gout_hbm, goutv, load_sem.at[1]),
        pltpu.make_async_copy(up_hbm, up.at[pl.ds(d * 1024, 1024)], load_sem.at[2]),
        pltpu.make_async_copy(down_hbm, down.at[pl.ds(d * 1024, 1024)], load_sem.at[3]),
    ]
    for copy in loads:
        copy.start()

    barrier = pltpu.get_barrier_semaphore()

    def greet(s, _):
        pl.semaphore_signal(barrier, inc=1, device_id=at_offset(s, 1), device_id_type=MESH)
        return 0

    for dev in (right_dev, left_dev, other_dev):
        pl.semaphore_signal(barrier, inc=1, device_id=dev, device_id_type=MESH)
    lax.fori_loop(1, NS, greet, 0)

    pos = pos_ref[...]
    gate = gate_ref[...]
    hot_near = lax.broadcasted_iota(jnp.int32, (NY * CAP, pos.shape[1]), 0) == pos
    hot_far = lax.broadcasted_iota(jnp.int32, ((NS - NY) * CAP, pos.shape[1]), 0) + NY * CAP == pos
    gate_near = jnp.sum(jnp.where(hot_near, gate, 0.0), axis=1, keepdims=True)
    gate_far = jnp.sum(jnp.where(hot_far, gate, 0.0), axis=1, keepdims=True)
    hot_near = hot_near.astype(BF16)
    hot_far = hot_far.astype(BF16)
    mine = pl.ds(pl.multiple_of(t * QUARTER, QUARTER), QUARTER)
    for part, buf in ((0, tokv), (1, goutv)):
        loads[part].wait()
        for q in range(4):
            placed = dot(hot_near, buf[:, q * QUARTER:(q + 1) * QUARTER], ((1,), (0,)))
            if part == 1:
                placed = placed * gate_near
            placed = placed.astype(BF16).reshape(NY, CAP, QUARTER)
            near[q, :, part] = placed
            rows[q, 0, part] = placed[0]
        placed = dot(hot_far, buf[:, mine], ((1,), (0,)))
        if part == 1:
            placed = placed * gate_far
        far[:, part] = placed.astype(BF16).reshape(NS - NY, CAP, QUARTER)

    pl.semaphore_wait(barrier, NS - 1 + 3)

    def send_near(s, _):
        remote(near.at[:, s], rows.at[:, s], near_send, yz_recv.at[0], at_offset(s, 1)).start()
        return 0

    def send_far(s, _):
        remote(far.at[s - NY], rows.at[t, s], far_send, yz_recv.at[s // NY], at_offset(s, 1)).start()
        return 0

    weights = []
    for i, (src, dst) in enumerate(((up_hbm, up), (down_hbm, down))):
        weights.append(remote(src, dst.at[pl.ds(d * 1024, 1024)], w_send.at[i], w_recv.at[i], other_dev))
    lax.fori_loop(1, NY, send_near, 0)
    lax.fori_loop(NY, NS, send_far, 0)
    for copy in weights:
        copy.start()

    def block(q, k, n=NY, skip=0):
        return rows.at[q, pl.ds(NY * k + skip, n)]

    def gather_own(k):
        mine = block(t, k)
        remote(mine, mine, far_send, yz_recv.at[k], left_dev).wait_recv()
        remote(mine, mine, own_send.at[0], plus_recv.at[k], right_dev).start()
        remote(mine, mine, own_send.at[1], minus_recv.at[k], left_dev).start()

    def gather_pass(k):
        got = block(left, k)
        remote(got, got, own_send.at[0], plus_recv.at[k], right_dev).wait_recv()
        half = block(left, k, 2)
        remote(half, half, fwd_send.at[0], fplus_recv.at[k], right_dev).start()
        got = block(right, k)
        remote(got, got, own_send.at[1], minus_recv.at[k], left_dev).wait_recv()
        half = block(right, k, 2, 2)
        remote(half, half, fwd_send.at[1], fminus_recv.at[k], left_dev).start()

    def gather_end(k):
        half = block(across, k, 2)
        remote(half, half, fwd_send.at[0], fplus_recv.at[k], right_dev).wait_recv()
        half = block(across, k, 2, 2)
        remote(half, half, fwd_send.at[1], fminus_recv.at[k], left_dev).wait_recv()

    def near_end():
        got = rows.at[:, pl.ds(1, NY - 1)]
        remote(got, got, near_send, yz_recv.at[0], left_dev).wait_recv()

    def products(p):
        part = pl.ds(8 * p, 8)
        span = pl.ds(128 * p, 128)
        remote(
            rows.at[pl.ds(2 * other, 2), part], prows.at[:, part], dp_send.at[0], prow_recv, other_dev
        ).start()
        for c in range(0, 1024, 256):
            cols = pl.ds(c, 256)
            pre = jnp.zeros((128, 256), F32)
            back = jnp.zeros((128, 256), F32)
            for q in range(4):
                depth = pl.ds(q * QUARTER, QUARTER)
                pre += dot(rows[q, part, 0].reshape(128, QUARTER), up[depth, cols], ((1,), (0,)))
                back += dot(rows[q, part, 1].reshape(128, QUARTER), down[depth, cols], ((1,), (0,)))
            hidden, slope = activation(pre, back)
            hs[0, span, cols] = hidden
            hs[1, span, cols] = slope
        remote(hs.at[:, span], phs.at[:, span], dp_send.at[1], phs_recv, other_dev).start()

    def input_share(p, q):
        span = pl.ds(128 * p, 128)
        depth = pl.ds(pl.multiple_of(q * QUARTER, QUARTER), QUARTER)
        inp[p, q] = dot(hs[1, span, :], up[depth, :], ((1,), (1,))).astype(BF16)

    def sum_first(p):
        input_share(p, across)
        remote(
            inp.at[p, across, pl.ds(0, 64)], ra.at[p], first_send.at[0], ra_recv.at[p], right_dev
        ).start()
        remote(
            inp.at[p, across, pl.ds(64, 64)], rb.at[p], first_send.at[1], rb_recv.at[p], left_dev
        ).start()
        input_share(p, right)
        input_share(p, left)
        input_share(p, t)

    def sum_second(p):
        remote(ra.at[p], ra.at[p], first_send.at[0], ra_recv.at[p], right_dev).wait_recv()
        top = pl.ds(0, 64)
        inp[p, right, top] = (inp[p, right, top].astype(F32) + ra[p].astype(F32)).astype(BF16)
        remote(inp.at[p, right], rp.at[p], second_send.at[0], rp_recv.at[p], right_dev).start()
        remote(rb.at[p], rb.at[p], first_send.at[1], rb_recv.at[p], left_dev).wait_recv()
        low = pl.ds(64, 64)
        inp[p, left, low] = (inp[p, left, low].astype(F32) + rb[p].astype(F32)).astype(BF16)
        remote(inp.at[p, left], rm.at[p], second_send.at[1], rm_recv.at[p], left_dev).start()

    def sum_last(p):
        remote(rp.at[p], rp.at[p], second_send.at[0], rp_recv.at[p], right_dev).wait_recv()
        remote(rm.at[p], rm.at[p], second_send.at[1], rm_recv.at[p], left_dev).wait_recv()
        total = inp[p, t].astype(F32) + rp[p].astype(F32) + rm[p].astype(F32)
        res[pl.ds(8 * p, 8)] = total.astype(BF16).reshape(8, CAP, QUARTER)

        def give_back(s, _):
            remote(res.at[s], ret.at[s], ret_send, ret_recv, at_offset(s, -1)).start()
            return 0

        lax.fori_loop(max(8 * p, 1), 8 * p + 8, give_back, 0)

    def weight_grads(which, q):
        out = gu if which == 0 else gd
        a = rows[2 * d + q, :, which].reshape(NS * CAP, QUARTER)
        b = prows[q, :, which].reshape(NS * CAP, QUARTER)
        for c in range(0, 1024, 256):
            cols = pl.ds(c, 256)
            total = dot(a, hs[1 - which, :, cols], ((0,), (0,)))
            total += dot(b, phs[1 - which, :, cols], ((0,), (0,)))
            out[pl.ds(q * QUARTER, QUARTER), cols] = total.astype(BF16)

    gather_own(1)
    for copy in loads[2:]:
        copy.wait()
    gather_own(2)
    gather_pass(1)
    for copy in weights:
        copy.wait_recv()
    near_end()
    gather_own(3)
    gather_pass(2)
    gather_end(1)
    products(0)
    sum_first(0)
    gather_own(4)
    gather_pass(3)
    gather_end(2)
    gather_end(3)
    products(1)
    sum_first(1)
    sum_second(0)
    gather_own(5)
    gather_pass(4)
    sum_second(1)
    sum_last(0)
    gather_own(6)
    gather_pass(5)
    gather_end(4)
    gather_end(5)
    products(2)
    sum_first(2)
    sum_last(1)
    gather_own(7)
    gather_pass(6)
    sum_second(2)
    gather_pass(7)
    sum_last(2)
    gather_end(6)
    gather_end(7)
    products(3)
    sum_first(3)
    remote(
        rows.at[pl.ds(0, 2)], prows, dp_send.at[0], prow_recv, other_dev
    ).wait_recv()
    remote(hs, phs, dp_send.at[1], phs_recv, other_dev).wait_recv()
    weight_grads(0, 0)
    sum_second(3)
    weight_grads(0, 1)
    copy_up = pltpu.make_async_copy(gu, gu_out, out_sem.at[0])
    copy_up.start()
    sum_last(3)
    weight_grads(1, 0)
    weight_grads(1, 1)
    copy_down = pltpu.make_async_copy(gd, gd_out, out_sem.at[1])
    copy_down.start()
    copy_own = pltpu.make_async_copy(res.at[0], ret.at[0], out_sem.at[2])
    copy_own.start()

    got = ret.at[pl.ds(1, NS - 1)]
    sent = res.at[pl.ds(1, NS - 1)]
    remote(sent, got, ret_send, ret_recv, left_dev).wait()
    remote(near.at[:, pl.ds(1, NY - 1)], rows.at[:, pl.ds(1, NY - 1)], near_send, yz_recv.at[0], left_dev).wait_send()
    remote(far, far, far_send, yz_recv.at[0], left_dev).wait_send()
    for i in range(2):
        own = rows.at[0, pl.ds(NY, NS - NY)]
        half = rows.at[0, pl.ds(NY, (NS - NY) // 2)]
        remote(own, own, own_send.at[i], plus_recv.at[0], left_dev).wait_send()
        remote(half, half, fwd_send.at[i], plus_recv.at[0], left_dev).wait_send()
        weights[i].wait_send()
        remote(ra, ra, first_send.at[i], ra_recv.at[0], left_dev).wait_send()
        remote(rp, rp, second_send.at[i], rp_recv.at[0], left_dev).wait_send()
    remote(prows, prows, dp_send.at[0], prow_recv, other_dev).wait_send()
    remote(hs, phs, dp_send.at[1], phs_recv, other_dev).wait_send()
    copy_up.wait()
    copy_down.wait()
    copy_own.wait()


def local(tokens, grad_output, gate_prob, expert_index, slot_index, up_weight, down_weight):
    count = tokens.shape[0]
    e = lax.axis_index("expert")
    y, z = e // NZ, e % NZ
    chosen = expert_index[:, 0]
    dy = (chosen // NZ - y + NY) % NY
    dz = (chosen % NZ - z + NZ) % NZ
    k = jnp.where(dz > NZ // 2, 2 * (NZ - dz), jnp.maximum(2 * dz - 1, 0))
    pos = (NY * k + dy) * CAP + slot_index[:, 0]
    vmem = pl.BlockSpec(memory_space=pltpu.VMEM)
    hbm = pl.BlockSpec(memory_space=pl.ANY)
    dma = pltpu.SemaphoreType.DMA
    shape = jax.ShapeDtypeStruct
    returned, grad_up, grad_down = pl.pallas_call(
        kernel,
        out_shape=(
            shape((NS, CAP, QUARTER), BF16),
            shape((1024, 1024), BF16),
            shape((1024, 1024), BF16),
        ),
        in_specs=[vmem, vmem, hbm, hbm, hbm, hbm],
        out_specs=(hbm, hbm, hbm),
        scratch_shapes=[
            pltpu.VMEM((count, 2048), BF16),
            pltpu.VMEM((count, 2048), BF16),
            pltpu.VMEM((4, NY, 2, CAP, QUARTER), BF16),
            pltpu.VMEM((NS - NY, 2, CAP, QUARTER), BF16),
            pltpu.VMEM((4, NS, 2, CAP, QUARTER), BF16),
            pltpu.VMEM((2, NS, 2, CAP, QUARTER), BF16),
            pltpu.VMEM((2048, 1024), BF16),
            pltpu.VMEM((2048, 1024), BF16),
            pltpu.VMEM((2, 512, 1024), BF16),
            pltpu.VMEM((2, 512, 1024), BF16),
            pltpu.VMEM((PAIRS, 4, 128, QUARTER), BF16),
            pltpu.VMEM((PAIRS, 64, QUARTER), BF16),
            pltpu.VMEM((PAIRS, 64, QUARTER), BF16),
            pltpu.VMEM((PAIRS, 128, QUARTER), BF16),
            pltpu.VMEM((PAIRS, 128, QUARTER), BF16),
            pltpu.VMEM((NS, CAP, QUARTER), BF16),
            pltpu.VMEM((1024, 1024), BF16),
            pltpu.VMEM((1024, 1024), BF16),
            dma((4,)), dma, dma, dma((NZ,)), dma((2,)), dma((NZ,)), dma((NZ,)), dma((2,)), dma((NZ,)), dma((NZ,)),
            dma((2,)), dma((2,)), dma((2,)), dma, dma,
            dma((2,)), dma((PAIRS,)), dma((PAIRS,)), dma((2,)), dma((PAIRS,)), dma((PAIRS,)), dma, dma, dma((3,)),
        ],
        compiler_params=pltpu.CompilerParams(
            collective_id=0, has_side_effects=True, vmem_limit_bytes=48 * 2**20
        ),
        cost_estimate=pl.CostEstimate(flops=11 * 10**9, bytes_accessed=12 * 2**20, transcendentals=2**19),
        name="expert_layer",
    )(pos[None, :], gate_prob[None, :], tokens, grad_output, up_weight[0], down_weight[0])
    onehot = (lax.broadcasted_iota(jnp.int32, (NS * CAP, count), 0) == pos[None, :]).astype(BF16)
    grad_tokens = dot(onehot, returned.reshape(NS * CAP, QUARTER), ((0,), (0,)))
    return grad_tokens.astype(BF16), grad_up[None], grad_down[None]


def solution(mesh):
    placed = (
        P(("expert", "dp"), None),
        P(("expert", "dp"), None),
        P(("expert", "dp")),
        P(("expert", "dp"), None),
        P(("expert", "dp"), None),
        P("expert", "dp", "tensor"),
        P("expert", "dp", "tensor"),
    )
    return jax.shard_map(
        local,
        mesh=mesh,
        in_specs=placed,
        out_specs=(
            P(("expert", "dp"), "tensor"),
            P("expert", "dp", "tensor"),
            P("expert", "dp", "tensor"),
        ),
        check_vma=False,
    )
```

time: 220 us -> 102 us (0.46)
  waiting for transfers between devices: 122 us -> 0 us
  Pallas kernels: 0 us -> 90.5 us
  matrix products: 34.8 us -> 1.06 us
  blocking collectives: 26.6 us -> 0 us
  starting transfers between devices: 18.3 us -> 0 us
  between operations: 13.9 us -> 0.67 us
  local copies, waits for them, and re-layouts: 2.81 us -> 6.79 us
    pallas_call x0 -> x1, Pallas kernels: none -> 90.5 us  [local(): pl.pallas_call(kernel, out_shape=(shape((NS, CAP, QUARTER), BF16), shape(...]
    all_to_all x2 -> x0, waiting for transfers between devices: 89.6 us -> none  [the longest x1 45.8 us: local(): lax.all_to_all(dispatch(tokens), 'expert', split_axis=0, concat_axis=0, t...]
    dot_general x8 -> x1, matrix products: 34.8 us -> 1.06 us  [dot(): return lax.dot_general(a, b, (dims, ((), ())), preferred_element_type=F32)]
    reduce_scatter x3 -> x0, waiting for transfers between devices: 31.1 us -> none  [the longest x1 16.1 us: local(): lax.psum_scatter(lax.dot_general(columns, hidden, (((0,), (0,)), ((), ())...]
    all_to_all x1 -> x0, blocking collectives: 26.6 us -> none  [local(): lax.all_to_all(share_sums, 'expert', split_axis=0, concat_axis=0, tiled=T...]
    all_to_all x2 -> x0, starting transfers between devices: 17.9 us -> none  [the longest x1 11.6 us: local(): lax.all_to_all(dispatch(tokens), 'expert', split_axis=0, concat_axis=0, t...]
    unnamed x14 -> x10, local copies, waits for them, and re-layouts: 2.81 us -> 6.79 us
  transfers between devices with their start and end apart: 7 -> 0, of which waited for: 4 -> 0; matrix products, arithmetic and copies ran while one was open for 11% -> 0% of each run, Pallas kernels for 0% -> 0%
where the time goes in v1:
time: 102 us; the launch traced here: 101 us
  Pallas kernels  90.5 us (89%)
  local copies, waits for them, and re-layouts  6.79 us (7%)
  other arithmetic  1.45 us (1%)
  matrix products  1.06 us (1%)
    pallas_call x1, Pallas kernels, local(): pl.pallas_call(kernel, out_shape=(shape((NS, CAP, QUARTER), BF16), shape(...  90.5 us
    unnamed x10, local copies, waits for them, and re-layouts  6.79 us

profile of v1, /device:TPU:4, one launch (start us, length us, event | category | flops | bytes accessed | tf_op | source)
XLA Modules:
  0.0 100.5 jit_solution(12610753112127335041)
XLA Ops:
  0.7 0.7 multiply_add_fusion
  1.4 0.7 bitcast_add_fusion.pos_ref
  2.1 0.0 copy-start
  2.1 1.2 %copy-done = bf16[256,2048]{1,0:T(8,128)(2,1)S(1)} copy-done((bf16[256,2048]{1,0:T(8,128)(2,1)S(1)}, bf16[256,2048]{1,0:T(8,128)(2,1)}, u32[]{:S(2)}) %copy-start) | copy-done | bytes 1048600
  3.3 0.0 copy-start.1
  3.3 1.2 %copy-done.1 = bf16[256,2048]{1,0:T(8,128)(2,1)S(1)} copy-done((bf16[256,2048]{1,0:T(8,128)(2,1)S(1)}, bf16[256,2048]{1,0:T(8,128)(2,1)}, u32[]{:S(2)}) %copy-start.1) | copy-done | bytes 1048600
  4.6 0.0 copy-start.2
  4.6 0.7 copy-done.2
  5.2 90.5 %expert_layer.1 = (bf16[32,16,512]{2,1,0:T(8,128)(2,1)S(1)}, bf16[1024,1024]{1,0:T(8,128)(2,1)S(1)}, bf16[1024,1024]{1,0:T(8,128)(2,1)}) custom-call(s32[1,256]{1,0:T(1,128)S(1)} %bitcast_add_fusion.pos_ref, f32[1,256]{1,0:T(1,128)S(1)} %bitcast.27, bf16[256,2048]{1,0:T(8,128)(2,1)S(1)} %copy-done, bf16[256,2048]{1,0:T(8,128)(2,1)S(1)} %copy-done.1, ...), custom_call_target="tpu_custom_call" | custom-call | flops 11000000512 | bytes 12582912 | tf_op jit(solution)/shard_map/expert_layer/pallas_call | solution.py:307
  95.8 1.1 %convolution_convert_fusion = bf16[256,512]{1,0:T(8,128)(2,1)} fusion(bf16[512,512]{1,0:T(8,128)(2,1)S(1)} %bitcast.28, s32[256]{0:T(256)S(1)} %multiply_add_fusion), kind=kOutput, calls=%fused_computation | convolution fusion | flops 134479872 | bytes 787456 | tf_op jit(solution)/shard_map/dot_general | solution.py:22
  96.8 0.0 copy-start.3
  96.8 1.3 %copy.12 = bf16[1,1024,1024]{2,1,0:T(8,128)(2,1)} copy(bf16[1,1024,1024]{2,1,0:T(8,128)(2,1)S(1)} %bitcast.26) | data formatting | bytes 4194304
  98.2 1.0 %copy-done.3 = bf16[1024,1024]{1,0:T(8,128)(2,1)S(1)} copy-done((bf16[1024,1024]{1,0:T(8,128)(2,1)S(1)}, bf16[1024,1024]{1,0:T(8,128)(2,1)}, u32[]{:S(2)}) %copy-start.3) | copy-done | bytes 2097176
  99.2 1.3 %copy.13 = bf16[1,1024,1024]{2,1,0:T(8,128)(2,1)} copy(bf16[1,1024,1024]{2,1,0:T(8,128)(2,1)S(1)} %bitcast.29) | data formatting | bytes 4194304
Async XLA Ops:
  2.1 1.2 %copy-start = (bf16[256,2048]{1,0:T(8,128)(2,1)S(1)}, bf16[256,2048]{1,0:T(8,128)(2,1)}, u32[]{:S(2)}) copy-start(bf16[256,2048]{1,0:T(8,128)(2,1)} %tok_hbm.1) | copy-start | bytes 3145732
  3.3 1.2 %copy-start.1 = (bf16[256,2048]{1,0:T(8,128)(2,1)S(1)}, bf16[256,2048]{1,0:T(8,128)(2,1)}, u32[]{:S(2)}) copy-start(bf16[256,2048]{1,0:T(8,128)(2,1)} %gout_hbm.1) | copy-start | bytes 3145732
  4.6 0.7 copy-start.2
  96.8 2.3 %copy-start.3 = (bf16[1024,1024]{1,0:T(8,128)(2,1)S(1)}, bf16[1024,1024]{1,0:T(8,128)(2,1)}, u32[]{:S(2)}) copy-start(bf16[1024,1024]{1,0:T(8,128)(2,1)} %get-tuple-element.8) | copy-start | bytes 6291460

commit v2 on v1

v2 whole, which is shorter than its diff:
```python
import jax
import jax.numpy as jnp
from jax import lax
from jax.experimental import pallas as pl
from jax.experimental.pallas import tpu as pltpu
from jax.sharding import PartitionSpec as P

MESH = pl.DeviceIdType.MESH
F32 = jnp.float32
BF16 = jnp.bfloat16
ROOT = 0.7978845608028654
CUBE = 0.044715

NY, NZ, NX = 4, 8, 4
CAP = 16
NS = NY * NZ
QUARTER = 512
PAIRS = 4
OFFSETS = (
    (0, 0), (1, 0), (3, 0), (2, 0),
    (0, 1), (0, -1), (1, 1), (3, -1),
    (2, 1), (2, -1), (3, 1), (1, -1),
    (0, 2), (0, -2), (1, 2), (1, -2),
    (2, 2), (2, -2), (3, 2), (3, -2),
    (0, 3), (0, -3), (1, 3), (1, -3),
    (2, 3), (2, -3), (3, 3), (3, -3),
    (0, 4), (1, 4), (2, 4), (3, 4),
)
NEAR = 8
SEND_ORDER = (2, 0, 1, 3, 4, 5, 6, 7)


def positions(expert, slot):
    e = lax.axis_index("expert")
    y, z = e // NZ, e % NZ
    code = (((expert >> 3) - y) & (NY - 1)) * NZ + (((expert & (NZ - 1)) - z) & (NZ - 1))
    place = jnp.zeros_like(code)
    for s, (dy, dz) in enumerate(OFFSETS):
        place = place + jnp.where(code == dy * NZ + dz % NZ, s, 0)
    return place * CAP + slot


def dot(a, b, dims):
    return lax.dot_general(a, b, (dims, ((), ())), preferred_element_type=F32)


def activation(pre, back):
    square = pre * pre
    bent = jnp.tanh(ROOT * (pre + CUBE * (pre * square)))
    share = 0.5 * (1.0 + bent)
    slope = share + pre * (0.5 * (1.0 - bent * bent)) * (ROOT * (1.0 + 3.0 * CUBE * square))
    return (pre * share).astype(BF16), (back * slope).astype(BF16)


def kernel(
    expert_hbm, slot_hbm, gate_hbm, tok_hbm, gout_hbm, up_hbm, down_hbm,
    ret, gu, gd,
    expert_ref, slot_ref, gate_ref, tokv, goutv, near, far, rows, prows, up, down, hs, phs, inp, ra, rb, rp, rm, res, gsum,
    load_sem, small_sem, near_send, far_send, yz_recv, own_send, plus_recv, minus_recv, fwd_send, fplus_recv, fminus_recv,
    w_send, w_recv, dp_send, prow_recv, phs_recv,
    first_send, ra_recv, rb_recv, second_send, rp_recv, rm_recv, ret_send, ret_recv,
):
    t = lax.axis_index("tensor")
    e = lax.axis_index("expert")
    d = lax.axis_index("dp")
    y, z = e // NZ, e % NZ
    left, right, across = (t + 3) % NX, (t + 1) % NX, (t + 2) % NX
    other = 1 - d

    def at_offset(s, sign):
        dy, dz = OFFSETS[s]
        return (t, ((y + sign * dy + NY) % NY) * NZ + (z + sign * dz + NZ) % NZ, d)

    right_dev, left_dev, other_dev = (right, e, d), (left, e, d), (t, e, other)

    def remote(src, dst, send, recv, dev):
        return pltpu.make_async_remote_copy(
            src_ref=src, dst_ref=dst, send_sem=send, recv_sem=recv, device_id=dev, device_id_type=MESH
        )

    loads = [
        pltpu.make_async_copy(tok_hbm, tokv, load_sem.at[0]),
        pltpu.make_async_copy(gout_hbm, goutv, load_sem.at[1]),
        pltpu.make_async_copy(up_hbm, up.at[pl.ds(d * 1024, 1024)], load_sem.at[2]),
        pltpu.make_async_copy(down_hbm, down.at[pl.ds(d * 1024, 1024)], load_sem.at[3]),
    ]
    small = [
        pltpu.make_async_copy(src, dst, small_sem.at[i])
        for i, (src, dst) in enumerate(((expert_hbm, expert_ref), (slot_hbm, slot_ref), (gate_hbm, gate_ref)))
    ]
    for copy in small + loads:
        copy.start()

    barrier = pltpu.get_barrier_semaphore()

    for dev in (right_dev, left_dev, other_dev):
        pl.semaphore_signal(barrier, inc=1, device_id=dev, device_id_type=MESH)
    for s in range(1, NS):
        pl.semaphore_signal(barrier, inc=1, device_id=at_offset(s, 1), device_id_type=MESH)

    for copy in small:
        copy.wait()
    pos = positions(expert_ref[...], slot_ref[...])
    gate = gate_ref[...]
    hot_near = lax.broadcasted_iota(jnp.int32, (NEAR * CAP, pos.shape[1]), 0) == pos
    hot_far = lax.broadcasted_iota(jnp.int32, ((NS - NEAR) * CAP, pos.shape[1]), 0) + NEAR * CAP == pos
    gate_near = jnp.sum(jnp.where(hot_near, gate, 0.0), axis=1, keepdims=True)
    gate_far = jnp.sum(jnp.where(hot_far, gate, 0.0), axis=1, keepdims=True)
    hot_near = hot_near.astype(BF16)
    hot_far = hot_far.astype(BF16)
    mine = pl.ds(pl.multiple_of(t * QUARTER, QUARTER), QUARTER)
    for part, buf in ((0, tokv), (1, goutv)):
        loads[part].wait()
        placed = dot(hot_far, buf[:, mine], ((1,), (0,)))
        if part == 1:
            placed = placed * gate_far
        far[:, part] = placed.astype(BF16).reshape(NS - NEAR, CAP, QUARTER)
        for q in range(4):
            placed = dot(hot_near, buf[:, q * QUARTER:(q + 1) * QUARTER], ((1,), (0,)))
            if part == 1:
                placed = placed * gate_near
            placed = placed.astype(BF16).reshape(NEAR, CAP, QUARTER)
            near[q, :, part] = placed
            rows[q, 0, part] = placed[0]

    pl.semaphore_wait(barrier, NS - 1 + 3)

    for g in SEND_ORDER:
        for s in range(max(4 * g, 1), 4 * g + 4):
            if s < NEAR:
                remote(near.at[:, s], rows.at[:, s], near_send, yz_recv.at[g], at_offset(s, 1)).start()
            else:
                remote(far.at[s - NEAR], rows.at[t, s], far_send, yz_recv.at[g], at_offset(s, 1)).start()
    weights = []
    for i, (src, dst) in enumerate(((up_hbm, up), (down_hbm, down))):
        weights.append(remote(src, dst.at[pl.ds(d * 1024, 1024)], w_send.at[i], w_recv.at[i], other_dev))
        weights[i].start()

    def block(q, k, n=NY, skip=0):
        return rows.at[q, pl.ds(NY * k + skip, n)]

    def gather_own(k):
        mine = block(t, k)
        remote(mine, mine, far_send, yz_recv.at[k], left_dev).wait_recv()
        remote(mine, mine, own_send.at[0], plus_recv.at[k], right_dev).start()
        remote(mine, mine, own_send.at[1], minus_recv.at[k], left_dev).start()

    def gather_pass(k):
        got = block(left, k)
        remote(got, got, own_send.at[0], plus_recv.at[k], right_dev).wait_recv()
        half = block(left, k, 2)
        remote(half, half, fwd_send.at[0], fplus_recv.at[k], right_dev).start()
        got = block(right, k)
        remote(got, got, own_send.at[1], minus_recv.at[k], left_dev).wait_recv()
        half = block(right, k, 2, 2)
        remote(half, half, fwd_send.at[1], fminus_recv.at[k], left_dev).start()

    def gather_end(k):
        half = block(across, k, 2)
        remote(half, half, fwd_send.at[0], fplus_recv.at[k], right_dev).wait_recv()
        half = block(across, k, 2, 2)
        remote(half, half, fwd_send.at[1], fminus_recv.at[k], left_dev).wait_recv()

    def near_end(g):
        got = rows.at[:, pl.ds(max(4 * g, 1), 4 * g + 4 - max(4 * g, 1))]
        remote(got, got, near_send, yz_recv.at[g], left_dev).wait_recv()

    def products(p, c):
        part = pl.ds(8 * p, 8)
        span = pl.ds(128 * p, 128)
        if c == 0:
            remote(
                rows.at[pl.ds(2 * other, 2), part], prows.at[:, part], dp_send.at[0], prow_recv.at[p], other_dev
            ).start()
        cols = pl.ds(256 * c, 256)
        pre = jnp.zeros((128, 256), F32)
        back = jnp.zeros((128, 256), F32)
        for q in range(4):
            depth = pl.ds(q * QUARTER, QUARTER)
            pre += dot(rows[q, part, 0].reshape(128, QUARTER), up[depth, cols], ((1,), (0,)))
            back += dot(rows[q, part, 1].reshape(128, QUARTER), down[depth, cols], ((1,), (0,)))
        hidden, slope = activation(pre, back)
        hs[0, span, cols] = hidden
        hs[1, span, cols] = slope
        if c == 3:
            remote(hs.at[:, span], phs.at[:, span], dp_send.at[1], phs_recv.at[p], other_dev).start()

    def input_share(p, q):
        span = pl.ds(128 * p, 128)
        depth = pl.ds(pl.multiple_of(q * QUARTER, QUARTER), QUARTER)
        inp[p, q] = dot(hs[1, span, :], up[depth, :], ((1,), (1,))).astype(BF16)

    def sum_first(p):
        input_share(p, across)
        remote(
            inp.at[p, across, pl.ds(0, 64)], ra.at[p], first_send.at[0], ra_recv.at[p], right_dev
        ).start()
        remote(
            inp.at[p, across, pl.ds(64, 64)], rb.at[p], first_send.at[1], rb_recv.at[p], left_dev
        ).start()
        input_share(p, right)
        input_share(p, left)
        input_share(p, t)

    def sum_second(p):
        remote(ra.at[p], ra.at[p], first_send.at[0], ra_recv.at[p], right_dev).wait_recv()
        top = pl.ds(0, 64)
        inp[p, right, top] = (inp[p, right, top].astype(F32) + ra[p].astype(F32)).astype(BF16)
        remote(inp.at[p, right], rp.at[p], second_send.at[0], rp_recv.at[p], right_dev).start()
        remote(rb.at[p], rb.at[p], first_send.at[1], rb_recv.at[p], left_dev).wait_recv()
        low = pl.ds(64, 64)
        inp[p, left, low] = (inp[p, left, low].astype(F32) + rb[p].astype(F32)).astype(BF16)
        remote(inp.at[p, left], rm.at[p], second_send.at[1], rm_recv.at[p], left_dev).start()

    def sum_last(p):
        remote(rp.at[p], rp.at[p], second_send.at[0], rp_recv.at[p], right_dev).wait_recv()
        remote(rm.at[p], rm.at[p], second_send.at[1], rm_recv.at[p], left_dev).wait_recv()
        total = inp[p, t].astype(F32) + rp[p].astype(F32) + rm[p].astype(F32)
        res[pl.ds(8 * p, 8)] = total.astype(BF16).reshape(8, CAP, QUARTER)

        if p == 0:
            ret[0] = total[:CAP].astype(BF16)
        for s in range(max(8 * p, 1), 8 * p + 8):
            remote(res.at[s], ret.at[s], ret_send, ret_recv, at_offset(s, -1)).start()

    def partner_rows(p):
        part = pl.ds(8 * p, 8)
        span = pl.ds(128 * p, 128)
        remote(
            rows.at[pl.ds(0, 2), part], prows.at[:, part], dp_send.at[0], prow_recv.at[p], other_dev
        ).wait_recv()
        remote(hs.at[:, span], phs.at[:, span], dp_send.at[1], phs_recv.at[p], other_dev).wait_recv()

    def weight_grads(half, which, q):
        out = gu if which == 0 else gd
        part = pl.ds(16 * half, 16)
        span = pl.ds(256 * half, 256)
        where = pl.ds(q * QUARTER, QUARTER)
        a = rows[2 * d + q, part, which].reshape(256, QUARTER)
        b = prows[q, part, which].reshape(256, QUARTER)
        for c in range(0, 1024, 256):
            cols = pl.ds(c, 256)
            total = dot(a, hs[1 - which, span, cols], ((0,), (0,)))
            total += dot(b, phs[1 - which, span, cols], ((0,), (0,)))
            if half == 0:
                gsum[which, where, cols] = total
            else:
                out[where, cols] = (gsum[which, where, cols] + total).astype(BF16)

    gather_own(2)
    for copy in loads[2:]:
        copy.wait()
    for copy in weights:
        copy.wait_recv()
    near_end(0)
    near_end(1)
    products(0, 0)
    products(0, 1)
    gather_pass(2)
    products(0, 2)
    products(0, 3)
    gather_own(3)
    sum_first(0)
    gather_own(4)
    gather_pass(3)
    sum_second(0)
    gather_end(2)
    gather_end(3)
    products(1, 0)
    products(1, 1)
    gather_pass(4)
    products(1, 2)
    products(1, 3)
    gather_own(5)
    sum_first(1)
    sum_last(0)
    gather_own(6)
    gather_pass(5)
    sum_second(1)
    gather_end(4)
    gather_end(5)
    products(2, 0)
    products(2, 1)
    gather_own(7)
    gather_pass(6)
    products(2, 2)
    products(2, 3)
    sum_first(2)
    sum_last(1)
    gather_pass(7)
    partner_rows(0)
    partner_rows(1)
    weight_grads(0, 0, 0)
    sum_second(2)
    gather_end(6)
    weight_grads(0, 0, 1)
    gather_end(7)
    products(3, 0)
    products(3, 1)
    products(3, 2)
    products(3, 3)
    sum_first(3)
    sum_last(2)
    weight_grads(0, 1, 0)
    sum_second(3)
    weight_grads(0, 1, 1)
    partner_rows(2)
    partner_rows(3)
    weight_grads(1, 0, 0)
    sum_last(3)
    weight_grads(1, 0, 1)
    weight_grads(1, 1, 0)
    weight_grads(1, 1, 1)

    got = ret.at[pl.ds(1, NS - 1)]
    sent = res.at[pl.ds(1, NS - 1)]
    remote(sent, got, ret_send, ret_recv, left_dev).wait()
    sent = near.at[:, pl.ds(1, NEAR - 1)]
    remote(sent, sent, near_send, yz_recv.at[0], left_dev).wait_send()
    remote(far, far, far_send, yz_recv.at[0], left_dev).wait_send()
    for i in range(2):
        own = rows.at[0, pl.ds(NEAR, NS - NEAR)]
        half = rows.at[0, pl.ds(NEAR, (NS - NEAR) // 2)]
        remote(own, own, own_send.at[i], plus_recv.at[0], left_dev).wait_send()
        remote(half, half, fwd_send.at[i], plus_recv.at[0], left_dev).wait_send()
        weights[i].wait_send()
        remote(ra, ra, first_send.at[i], ra_recv.at[0], left_dev).wait_send()
        remote(rp, rp, second_send.at[i], rp_recv.at[0], left_dev).wait_send()
    remote(prows, prows, dp_send.at[0], prow_recv.at[0], other_dev).wait_send()
    remote(hs, phs, dp_send.at[1], phs_recv.at[0], other_dev).wait_send()


def finish(expert_hbm, slot_hbm, ret, gu, gd, gt_out, gu_out, gd_out, expert_ref, slot_ref, gt, sems):
    small = [
        pltpu.make_async_copy(expert_hbm, expert_ref, sems.at[5]),
        pltpu.make_async_copy(slot_hbm, slot_ref, sems.at[6]),
    ]
    stores = []
    for i in range(4):
        src, dst = ((gu, gu_out), (gd, gd_out))[i // 2]
        where = pl.ds(QUARTER * (i % 2), QUARTER)
        stores.append(pltpu.make_async_copy(src.at[where], dst.at[where], sems.at[i]))
    for copy in small + stores:
        copy.start()
    for copy in small:
        copy.wait()
    pos = positions(expert_ref[...], slot_ref[...])
    onehot = (lax.broadcasted_iota(jnp.int32, (NS * CAP, pos.shape[1]), 0) == pos).astype(BF16)
    gt[...] = dot(onehot, ret[...].reshape(NS * CAP, QUARTER), ((0,), (0,))).astype(BF16)
    stores.append(pltpu.make_async_copy(gt, gt_out, sems.at[4]))
    stores[4].start()
    for copy in stores:
        copy.wait()


def local(tokens, grad_output, gate_prob, expert_index, slot_index, up_weight, down_weight):
    count = tokens.shape[0]
    expert, slot, gate, tokens, grad_output, up, down = (
        pltpu.with_memory_space_constraint(a, pltpu.HBM)
        for a in (
            expert_index.reshape(1, count), slot_index.reshape(1, count), gate_prob.reshape(1, count),
            tokens, grad_output, up_weight[0], down_weight[0],
        )
    )
    vmem = pl.BlockSpec(memory_space=pltpu.VMEM)
    hbm = pl.BlockSpec(memory_space=pltpu.HBM)
    dma = pltpu.SemaphoreType.DMA
    shape = jax.ShapeDtypeStruct
    returned, grad_up, grad_down = pl.pallas_call(
        kernel,
        out_shape=(
            shape((NS, CAP, QUARTER), BF16),
            shape((1024, 1024), BF16),
            shape((1024, 1024), BF16),
        ),
        in_specs=[hbm] * 7,
        out_specs=(vmem, vmem, vmem),
        scratch_shapes=[
            pltpu.VMEM((1, count), jnp.int32),
            pltpu.VMEM((1, count), jnp.int32),
            pltpu.VMEM((1, count), F32),
            pltpu.VMEM((count, 2048), BF16),
            pltpu.VMEM((count, 2048), BF16),
            pltpu.VMEM((4, NEAR, 2, CAP, QUARTER), BF16),
            pltpu.VMEM((NS - NEAR, 2, CAP, QUARTER), BF16),
            pltpu.VMEM((4, NS, 2, CAP, QUARTER), BF16),
            pltpu.VMEM((2, NS, 2, CAP, QUARTER), BF16),
            pltpu.VMEM((2048, 1024), BF16),
            pltpu.VMEM((2048, 1024), BF16),
            pltpu.VMEM((2, 512, 1024), BF16),
            pltpu.VMEM((2, 512, 1024), BF16),
            pltpu.VMEM((PAIRS, 4, 128, QUARTER), BF16),
            pltpu.VMEM((PAIRS, 64, QUARTER), BF16),
            pltpu.VMEM((PAIRS, 64, QUARTER), BF16),
            pltpu.VMEM((PAIRS, 128, QUARTER), BF16),
            pltpu.VMEM((PAIRS, 128, QUARTER), BF16),
            pltpu.VMEM((NS, CAP, QUARTER), BF16),
            pltpu.VMEM((2, 1024, 1024), F32),
            dma((4,)), dma((3,)), dma, dma, dma((NZ,)), dma((2,)), dma((NZ,)), dma((NZ,)), dma((2,)), dma((NZ,)), dma((NZ,)),
            dma((2,)), dma((2,)), dma((2,)), dma((PAIRS,)), dma((PAIRS,)),
            dma((2,)), dma((PAIRS,)), dma((PAIRS,)), dma((2,)), dma((PAIRS,)), dma((PAIRS,)), dma, dma,
        ],
        compiler_params=pltpu.CompilerParams(
            collective_id=0, has_side_effects=True, vmem_limit_bytes=44 * 2**20
        ),
        cost_estimate=pl.CostEstimate(flops=11 * 10**9, bytes_accessed=12 * 2**20, transcendentals=2**19),
        name="expert_layer",
    )(expert, slot, gate, tokens, grad_output, up, down)
    grad_tokens, grad_up, grad_down = pl.pallas_call(
        finish,
        out_shape=(
            shape((count, QUARTER), BF16),
            shape((1024, 1024), BF16),
            shape((1024, 1024), BF16),
        ),
        in_specs=[hbm, hbm, vmem, vmem, vmem],
        out_specs=(hbm, hbm, hbm),
        scratch_shapes=[
            pltpu.VMEM((1, count), jnp.int32),
            pltpu.VMEM((1, count), jnp.int32),
            pltpu.VMEM((count, QUARTER), BF16),
            dma((7,)),
        ],
        compiler_params=pltpu.CompilerParams(vmem_limit_bytes=16 * 2**20),
        name="finish",
    )(expert, slot, returned, grad_up, grad_down)
    return grad_tokens, grad_up[None], grad_down[None]


def solution(mesh):
    placed = (
        P(("expert", "dp"), None),
        P(("expert", "dp"), None),
        P(("expert", "dp")),
        P(("expert", "dp"), None),
        P(("expert", "dp"), None),
        P("expert", "dp", "tensor"),
        P("expert", "dp", "tensor"),
    )
    return jax.shard_map(
        local,
        mesh=mesh,
        in_specs=placed,
        out_specs=(
            P(("expert", "dp"), "tensor"),
            P("expert", "dp", "tensor"),
            P("expert", "dp", "tensor"),
        ),
        check_vma=False,
    )
```

time: 102 us -> 83.1 us (0.81)
  Pallas kernels: 90.5 us -> 81.5 us
  local copies, waits for them, and re-layouts: 6.79 us -> 0 us
  other arithmetic: 1.45 us -> 0 us
  matrix products: 1.06 us -> 0 us
    pallas_call x1, Pallas kernels: 90.5 us -> 79.4 us  [local(): pl.pallas_call(kernel, out_shape=(shape((NS, CAP, QUARTER), BF16), shape(...]
    unnamed x10 -> x0, local copies, waits for them, and re-layouts: 6.79 us -> none
    pallas_call x0 -> x1, Pallas kernels: none -> 2.15 us  [local(): pl.pallas_call(finish, out_shape=(shape((count, QUARTER), BF16), shape((1...]
    add x2 -> x0, other arithmetic: 1.45 us -> none  [local(): pos = (NY * k + dy) * CAP + slot_index[:, 0]]
    dot_general x1 -> x0, matrix products: 1.06 us -> none  [dot(): return lax.dot_general(a, b, (dims, ((), ())), preferred_element_type=F32)]
where the time goes in v2:
time: 83.1 us; the launch traced here: 82.3 us
  Pallas kernels  81.5 us (98%)
    pallas_call x1, Pallas kernels, local(): pl.pallas_call(kernel, out_shape=(shape((NS, CAP, QUARTER), BF16), shape(...  79.4 us
    pallas_call x1, Pallas kernels, local(): pl.pallas_call(finish, out_shape=(shape((count, QUARTER), BF16), shape((1...  2.15 us

profile of v2, /device:TPU:4, one launch (start us, length us, event | category | flops | bytes accessed | tf_op | source)
XLA Modules:
  0.0 82.3 jit_solution(12355665889321773541)
XLA Ops:
  0.6 79.4 %expert_layer.1 = (bf16[32,16,512]{2,1,0:T(8,128)(2,1)S(1)}, bf16[1024,1024]{1,0:T(8,128)(2,1)S(1)}, bf16[1024,1024]{1,0:T(8,128)(2,1)S(1)}) custom-call(s32[1,256]{1,0:T(1,128)} %bitcast.7, s32[1,256]{1,0:T(1,128)} %bitcast.9, f32[1,256]{1,0:T(1,128)} %bitcast.15, bf16[256,2048]{1,0:T(8,128)(2,1)} %tok_hbm.1, bf16[256,2048]{1,0:T(8,128)(2,1)} %gout_hbm.1, ...), custom_call_target="tpu_custom_call" | custom-call | flops 11000000512 | bytes 12582912 | tf_op jit(solution)/shard_map/expert_layer/pallas_call | solution.py:369
  80.0 2.1 %finish.1 = (bf16[256,512]{1,0:T(8,128)(2,1)}, bf16[1024,1024]{1,0:T(8,128)(2,1)}, bf16[1024,1024]{1,0:T(8,128)(2,1)}) custom-call(s32[1,256]{1,0:T(1,128)} %bitcast.8, s32[1,256]{1,0:T(1,128)} %bitcast.10, bf16[32,16,512]{2,1,0:T(8,128)(2,1)S(1)} %get-tuple-element.9.ret, bf16[1024,1024]{1,0:T(8,128)(2,1)S(1)} %get-tuple-element.10.gu, ...), custom_call_target="tpu_custom_call" | custom-call | tf_op jit(solution)/shard_map/finish/pallas_call | solution.py:409

commit v3 on v2

--- a/solution.py
+++ b/solution.py
@@ -27,7 +27,7 @@
     (0, 4), (1, 4), (2, 4), (3, 4),
 )
 NEAR = 8
-SEND_ORDER = (2, 0, 1, 3, 4, 5, 6, 7)
+SEND_ORDER = (2, 0, 3, 4, 5, 6, 7, 1)
 
 
 def positions(expert, slot):
@@ -88,7 +88,7 @@
         pltpu.make_async_copy(src, dst, small_sem.at[i])
         for i, (src, dst) in enumerate(((expert_hbm, expert_ref), (slot_hbm, slot_ref), (gate_hbm, gate_ref)))
     ]
-    for copy in small + loads:
+    for copy in small + loads[:2]:
         copy.start()
 
     barrier = pltpu.get_barrier_semaphore()
@@ -123,6 +123,8 @@
             near[q, :, part] = placed
             rows[q, 0, part] = placed[0]
 
+    for copy in loads[2:]:
+        copy.start()
     pl.semaphore_wait(barrier, NS - 1 + 3)
 
     for g in SEND_ORDER:
@@ -233,81 +235,78 @@
 
     def weight_grads(half, which, q):
         out = gu if which == 0 else gd
-        part = pl.ds(16 * half, 16)
-        span = pl.ds(256 * half, 256)
         where = pl.ds(q * QUARTER, QUARTER)
-        a = rows[2 * d + q, part, which].reshape(256, QUARTER)
-        b = prows[q, part, which].reshape(256, QUARTER)
+        factors = []
+        for p in ((1, 2), (3, 0))[half]:
+            part = pl.ds(8 * p, 8)
+            span = pl.ds(128 * p, 128)
+            factors.append((rows[2 * d + q, part, which].reshape(128, QUARTER), hs, span))
+            factors.append((prows[q, part, which].reshape(128, QUARTER), phs, span))
+        left_factor = jnp.concatenate([rows for rows, _, _ in factors], axis=0)
         for c in range(0, 1024, 256):
             cols = pl.ds(c, 256)
-            total = dot(a, hs[1 - which, span, cols], ((0,), (0,)))
-            total += dot(b, phs[1 - which, span, cols], ((0,), (0,)))
+            right_factor = jnp.concatenate([ref[1 - which, span, cols] for _, ref, span in factors], axis=0)
+            total = dot(left_factor, right_factor, ((0,), (0,)))
             if half == 0:
                 gsum[which, where, cols] = total
             else:
                 out[where, cols] = (gsum[which, where, cols] + total).astype(BF16)
 
     gather_own(2)
+    gather_pass(2)
     for copy in loads[2:]:
         copy.wait()
     for copy in weights:
         copy.wait_recv()
-    near_end(0)
-    near_end(1)
-    products(0, 0)
-    products(0, 1)
-    gather_pass(2)
-    products(0, 2)
-    products(0, 3)
     gather_own(3)
-    sum_first(0)
     gather_own(4)
     gather_pass(3)
-    sum_second(0)
+    gather_pass(4)
     gather_end(2)
     gather_end(3)
-    products(1, 0)
-    products(1, 1)
-    gather_pass(4)
-    products(1, 2)
-    products(1, 3)
+    for c in range(4):
+        products(1, c)
     gather_own(5)
+    gather_own(6)
     sum_first(1)
-    sum_last(0)
-    gather_own(6)
     gather_pass(5)
     sum_second(1)
+    gather_pass(6)
     gather_end(4)
     gather_end(5)
     products(2, 0)
     products(2, 1)
     gather_own(7)
-    gather_pass(6)
     products(2, 2)
     products(2, 3)
     sum_first(2)
     sum_last(1)
     gather_pass(7)
-    partner_rows(0)
+    sum_second(2)
     partner_rows(1)
+    partner_rows(2)
     weight_grads(0, 0, 0)
-    sum_second(2)
     gather_end(6)
-    weight_grads(0, 0, 1)
     gather_end(7)
-    products(3, 0)
-    products(3, 1)
-    products(3, 2)
-    products(3, 3)
+    for c in range(4):
+        products(3, c)
     sum_first(3)
     sum_last(2)
+    near_end(0)
+    near_end(1)
+    for c in range(4):
+        products(0, c)
+    sum_second(3)
+    sum_first(0)
+    weight_grads(0, 0, 1)
     weight_grads(0, 1, 0)
-    sum_second(3)
+    sum_second(0)
+    sum_last(3)
     weight_grads(0, 1, 1)
-    partner_rows(2)
     partner_rows(3)
+    partner_rows(0)
     weight_grads(1, 0, 0)
-    sum_last(3)
+    sum_last(0)
     weight_grads(1, 0, 1)
     weight_grads(1, 1, 0)
     weight_grads(1, 1, 1)

time: 83.1 us -> 80.4 us (0.968)
  Pallas kernels: 81.5 us -> 79.5 us
    pallas_call x1, Pallas kernels: 79.4 us -> 77.3 us  [local(): pl.pallas_call(kernel, out_shape=(shape((NS, CAP, QUARTER), BF16), shape(...]
where the time goes in v3:
time: 80.4 us; the launch traced here: 80.3 us
  Pallas kernels  79.5 us (99%)
    pallas_call x1, Pallas kernels, local(): pl.pallas_call(kernel, out_shape=(shape((NS, CAP, QUARTER), BF16), shape(...  77.3 us
    pallas_call x1, Pallas kernels, local(): pl.pallas_call(finish, out_shape=(shape((count, QUARTER), BF16), shape((1...  2.15 us

profile of v3, /device:TPU:4, one launch (start us, length us, event | category | flops | bytes accessed | tf_op | source)
XLA Modules:
  0.0 80.3 jit_solution(17716904797096479046)
XLA Ops:
  0.6 77.3 %expert_layer.1 = (bf16[32,16,512]{2,1,0:T(8,128)(2,1)S(1)}, bf16[1024,1024]{1,0:T(8,128)(2,1)S(1)}, bf16[1024,1024]{1,0:T(8,128)(2,1)S(1)}) custom-call(s32[1,256]{1,0:T(1,128)} %bitcast.7, s32[1,256]{1,0:T(1,128)} %bitcast.9, f32[1,256]{1,0:T(1,128)} %bitcast.15, bf16[256,2048]{1,0:T(8,128)(2,1)} %tok_hbm.1, bf16[256,2048]{1,0:T(8,128)(2,1)} %gout_hbm.1, ...), custom_call_target="tpu_custom_call" | custom-call | flops 11000000512 | bytes 12582912 | tf_op jit(solution)/shard_map/expert_layer/pallas_call | solution.py:368
  78.0 2.1 %finish.1 = (bf16[256,512]{1,0:T(8,128)(2,1)}, bf16[1024,1024]{1,0:T(8,128)(2,1)}, bf16[1024,1024]{1,0:T(8,128)(2,1)}) custom-call(s32[1,256]{1,0:T(1,128)} %bitcast.8, s32[1,256]{1,0:T(1,128)} %bitcast.10, bf16[32,16,512]{2,1,0:T(8,128)(2,1)S(1)} %get-tuple-element.9.ret, bf16[1024,1024]{1,0:T(8,128)(2,1)S(1)} %get-tuple-element.10.gu, ...), custom_call_target="tpu_custom_call" | custom-call | tf_op jit(solution)/shard_map/finish/pallas_call | solution.py:408

commit v4 on v3

--- a/solution.py
+++ b/solution.py
@@ -200,6 +200,8 @@
         remote(
             inp.at[p, across, pl.ds(64, 64)], rb.at[p], first_send.at[1], rb_recv.at[p], left_dev
         ).start()
+
+    def sum_rest(p):
         input_share(p, right)
         input_share(p, left)
         input_share(p, t)
@@ -270,6 +272,7 @@
     gather_own(6)
     sum_first(1)
     gather_pass(5)
+    sum_rest(1)
     sum_second(1)
     gather_pass(6)
     gather_end(4)
@@ -280,8 +283,9 @@
     products(2, 2)
     products(2, 3)
     sum_first(2)
+    gather_pass(7)
+    sum_rest(2)
     sum_last(1)
-    gather_pass(7)
     sum_second(2)
     partner_rows(1)
     partner_rows(2)
@@ -291,13 +295,17 @@
     for c in range(4):
         products(3, c)
     sum_first(3)
+    sum_rest(3)
     sum_last(2)
     near_end(0)
     near_end(1)
-    for c in range(4):
-        products(0, c)
+    products(0, 0)
+    products(0, 1)
     sum_second(3)
+    products(0, 2)
+    products(0, 3)
     sum_first(0)
+    sum_rest(0)
     weight_grads(0, 0, 1)
     weight_grads(0, 1, 0)
     sum_second(0)

time: 80.4 us -> 80.1 us (level)
  no operation moved by 1% of the time
where the time goes in v4:
time: 80.1 us; the launch traced here: 79.9 us
  Pallas kernels  79.1 us (99%)
    pallas_call x1, Pallas kernels, local(): pl.pallas_call(kernel, out_shape=(shape((NS, CAP, QUARTER), BF16), shape(...  77 us
    pallas_call x1, Pallas kernels, local(): pl.pallas_call(finish, out_shape=(shape((count, QUARTER), BF16), shape((1...  2.15 us

profile of v4, /device:TPU:4, one launch (start us, length us, event | category | flops | bytes accessed | tf_op | source)
XLA Modules:
  0.0 79.9 jit_solution(2976853959624838621)
XLA Ops:
  0.6 77.0 %expert_layer.1 = (bf16[32,16,512]{2,1,0:T(8,128)(2,1)S(1)}, bf16[1024,1024]{1,0:T(8,128)(2,1)S(1)}, bf16[1024,1024]{1,0:T(8,128)(2,1)S(1)}) custom-call(s32[1,256]{1,0:T(1,128)} %bitcast.7, s32[1,256]{1,0:T(1,128)} %bitcast.9, f32[1,256]{1,0:T(1,128)} %bitcast.15, bf16[256,2048]{1,0:T(8,128)(2,1)} %tok_hbm.1, bf16[256,2048]{1,0:T(8,128)(2,1)} %gout_hbm.1, ...), custom_call_target="tpu_custom_call" | custom-call | flops 11000000512 | bytes 12582912 | tf_op jit(solution)/shard_map/expert_layer/pallas_call | solution.py:376
  77.6 2.1 %finish.1 = (bf16[256,512]{1,0:T(8,128)(2,1)}, bf16[1024,1024]{1,0:T(8,128)(2,1)}, bf16[1024,1024]{1,0:T(8,128)(2,1)}) custom-call(s32[1,256]{1,0:T(1,128)} %bitcast.8, s32[1,256]{1,0:T(1,128)} %bitcast.10, bf16[32,16,512]{2,1,0:T(8,128)(2,1)S(1)} %get-tuple-element.9.ret, bf16[1024,1024]{1,0:T(8,128)(2,1)S(1)} %get-tuple-element.10.gu, ...), custom_call_target="tpu_custom_call" | custom-call | tf_op jit(solution)/shard_map/finish/pallas_call | solution.py:416
